TPU v7x, 32 devices: a whole 2x2x4 slice. The times are simulated.
32 devices in a mesh: gx: 4 (over y, core), gy: 8 (over z, x).
Axes of the slice: x: 2, y: 2, z: 4, core: 2. Of those that a mesh axis runs over, the one named last changes fastest.
Arguments:
- start_vector: float32 [2, 16, 64, 1024], P(None, None, 'gx', 'gy'), may hold values from -6 to 6
- viscosity: float32 [16, 64, 1024], P(None, 'gx', 'gy'), may hold values from 0.1 to 10
- friction: float32 [16, 64, 1024], P(None, 'gx', 'gy'), may hold values from 0.5 to 5
- shifts: float32 [8], replicated, may hold values from 0.2 to 1.6, as said below
Outputs:
- orthonormal: float32 [9, 2, 16, 64, 1024], P(None, None, None, 'gx', 'gy')
- factor: float32 [9, 9], replicated
Inputs may be any that keep to these rules, and one draw needn't show every extreme that they name: The 8 shifts are distinct, one in each of 8 equal parts of the range.
All inputs are finite; a program needn't handle non-finite values.
Results may differ from a plain program's by a relative error of at most 0.00035.
Values sent between devices are 32-bit elements; how exact they have to be, the bound alone decides.
A program may use at most 128 MiB of HBM per device.

v0:
```python
import jax
import jax.numpy as jnp
from jax import lax
from jax.sharding import PartitionSpec as P

cross_gain = 1.0


def extended(shard, sides, width):
    for axis, dim in sides:
        peers, length = (lax.axis_size(axis), shard.shape[dim])
        up = [(i, (i + 1) % peers) for i in range(peers - 1)]
        down = [(j, i) for i, j in up]
        last = lax.slice_in_dim(shard, length - width, length, axis=dim)
        first = lax.slice_in_dim(shard, 0, width, axis=dim)
        before = lax.ppermute(last, axis, up)
        after = lax.ppermute(first, axis, down)
        shard = jnp.concatenate([before, shard, after], axis=dim)
    return shard


def neighbour_offsets():
    offsets = []
    for shift_z in (-1, 0, 1):
        for shift_x in (-1, 0, 1):
            for shift_y in (-1, 0, 1):
                distance = abs(shift_z) + abs(shift_x) + abs(shift_y)
                if distance == 0:
                    continue
                offsets.append((shift_z, shift_x, shift_y, 0.5 ** (distance - 1)))
    return offsets


def apply_operator(field_pad, eta_pad, friction, region_mask):
    levels = friction.shape[0]
    row_count = field_pad.shape[2] - 2
    col_count = field_pad.shape[3] - 2
    eta_z = jnp.pad(eta_pad, ((1, 1), (0, 0), (0, 0)))
    field_z = jnp.pad(field_pad, ((0, 0), (1, 1), (0, 0), (0, 0)))
    centre_eta = eta_pad[:, 1 : 1 + row_count, 1 : 1 + col_count]
    diagonal = friction
    summed = jnp.zeros((2, levels, row_count, col_count), jnp.float32)
    for shift_z, shift_x, shift_y, weight in neighbour_offsets():
        linkage = (
            weight
            * 0.5
            * (
                centre_eta
                + eta_z[
                    1 + shift_z : 1 + shift_z + levels,
                    1 + shift_x : 1 + shift_x + row_count,
                    1 + shift_y : 1 + shift_y + col_count,
                ]
            )
        )
        diagonal = diagonal + linkage
        summed = (
            summed
            + linkage[None]
            * field_z[
                :,
                1 + shift_z : 1 + shift_z + levels,
                1 + shift_x : 1 + shift_x + row_count,
                1 + shift_y : 1 + shift_y + col_count,
            ]
        )
    crossed = 0.25 * (
        field_pad[:, :, 2 : 2 + row_count, 2 : 2 + col_count]
        - field_pad[:, :, 2 : 2 + row_count, 0:col_count]
        - field_pad[:, :, 0:row_count, 2 : 2 + col_count]
        + field_pad[:, :, 0:row_count, 0:col_count]
    )
    centre = field_pad[:, :, 1 : 1 + row_count, 1 : 1 + col_count]
    safe_diag = jnp.where(region_mask > 0, diagonal, 1.0)
    result = centre - (summed - cross_gain * centre_eta[None] * crossed[::-1]) / safe_diag
    return result * region_mask


def lower_inverse(factor_low):
    order_n = factor_low.shape[0]
    identity = jnp.eye(order_n, dtype=jnp.float32)
    inverse = jnp.zeros((order_n, order_n), jnp.float32)
    for position in range(order_n):
        earlier = jnp.dot(
            factor_low[position, :position], inverse[:position], precision=lax.Precision.HIGHEST
        )
        inverse = inverse.at[position].set(
            (identity[position] - earlier) / factor_low[position, position]
        )
    return inverse


def cholesky_pass(basis_rows, gram):
    factor_low = jnp.linalg.cholesky(gram)
    return (
        jnp.dot(lower_inverse(factor_low), basis_rows, precision=lax.Precision.HIGHEST),
        factor_low,
    )


def on_device(start_vector, viscosity, friction, shifts):
    levels, row_count, col_count = viscosity.shape
    powers = shifts.shape[0]
    total_count = 2 * levels * row_count * lax.axis_size("gx") * col_count * lax.axis_size("gy")
    krylov = [start_vector]
    coeffs = jnp.stack([viscosity, friction])
    widened = extended(coeffs, (("gx", 2), ("gy", 3)), powers + 1)
    current = extended(start_vector, (("gx", 2), ("gy", 3)), powers)
    row_pos = (
        lax.axis_index("gx") * row_count - (powers + 1) + jnp.arange(row_count + 2 * powers + 2)
    )
    col_pos = (
        lax.axis_index("gy") * col_count - (powers + 1) + jnp.arange(col_count + 2 * powers + 2)
    )
    row_in = (row_pos >= 0) & (row_pos < row_count * lax.axis_size("gx"))
    col_in = (col_pos >= 0) & (col_pos < col_count * lax.axis_size("gy"))
    inside = (row_in[:, None] & col_in[None, :]).astype(jnp.float32)
    for power in range(powers):
        margin = powers - power
        eta_pad = widened[0][
            :,
            power + 1 : power + 1 + row_count + 2 * margin,
            power + 1 : power + 1 + col_count + 2 * margin,
        ]
        fric_part = widened[1][
            :,
            power + 2 : power + row_count + 2 * margin,
            power + 2 : power + col_count + 2 * margin,
        ]
        region = inside[
            power + 2 : power + row_count + 2 * margin, power + 2 : power + col_count + 2 * margin
        ]
        applied = apply_operator(current, eta_pad, fric_part, region)
        current = applied - shifts[power] * current[:, :, 1:-1, 1:-1]
        krylov.append(
            current[:, :, margin - 1 : margin - 1 + row_count, margin - 1 : margin - 1 + col_count]
        )

    def global_gram(basis_rows):
        partial_value = jnp.dot(basis_rows, basis_rows.T, precision=lax.Precision.HIGHEST)
        summed = lax.psum(partial_value, ("gx", "gy"))
        return summed / total_count

    basis_rows = jnp.stack(krylov).reshape(powers + 1, -1)
    ortho_one, low_one = cholesky_pass(basis_rows, global_gram(basis_rows))
    ortho_two, low_two = cholesky_pass(ortho_one, global_gram(ortho_one))
    factor = jnp.dot(low_two.T, low_one.T, precision=lax.Precision.HIGHEST)
    return (ortho_two.reshape(powers + 1, 2, levels, row_count, col_count), factor)


def solution(mesh):
    return jax.shard_map(
        on_device,
        mesh=mesh,
        in_specs=(P(None, None, "gx", "gy"), P(None, "gx", "gy"), P(None, "gx", "gy"), P()),
        out_specs=(P(None, None, None, "gx", "gy"), P()),
        check_vma=False,
    )
```

profile of v0, /device:TPU:0, one launch (start us, length us, event | category | flops | bytes accessed | tf_op | source)
XLA Modules:
  0.0 433.7 jit_solution(16997418263096803367)
XLA Ops:
  1.6 2.4 collective-permute-start
  8.0 5.8 %collective-permute-start.4 = (f32[2,16,9,128]{3,1,2,0:T(8,128)S(1)}, f32[2,16,9,128]{3,1,2,0:T(8,128)S(1)}, u32[]{:S(2)}, u32[]{:S(2)}) collective-permute-start(f32[2,16,9,128]{3,1,2,0:T(8,128)S(1)} %copy.750), channel_id=1, source_target_pairs={{0,8},{8,16},{16,24},{1,9},{9,17},{17,25},{2,10},{10,18},{18,26},{... | collective-permute-start | bytes 442376 | tf_op jit(solution)/shard_map/ppermute | solution.py:16
  23.9 2.0 copy.507
  29.2 5.3 %collective-permute-start.2 = (f32[2,16,32,8]{3,2,1,0:T(8,128)}, f32[2,16,32,8]{3,2,1,0:T(8,128)}, u32[]{:S(2)}, u32[]{:S(2)}) collective-permute-start(f32[2,16,32,8]{3,2,1,0:T(8,128)} %get-tuple-element.459), channel_id=1, source_target_pairs={{0,1},{1,2},{2,3},{3,4},{4,5},{5,6},{6,7},{8,9},{9,10},{10,11},{11... | collective-permute-start | bytes 98312 | tf_op jit(solution)/shard_map/ppermute | solution.py:16
  34.5 2.1 copy.508
  36.6 2.2 copy.506
  38.8 4.0 pad_maximum_fusion
  46.6 5.2 %collective-permute-start.6 = (f32[2,16,34,9]{2,1,3,0:T(8,128)}, f32[2,16,34,9]{2,1,3,0:T(8,128)}, u32[]{:S(2)}, u32[]{:S(2)}) collective-permute-start(f32[2,16,34,9]{2,1,3,0:T(8,128)} %get-tuple-element.439), channel_id=1, source_target_pairs={{0,1},{1,2},{2,3},{3,4},{4,5},{5,6},{6,7},{8,9},{9,10},{10,11},{11... | collective-permute-start | bytes 117512 | tf_op jit(solution)/shard_map/ppermute | solution.py:16
  51.8 7.3 %collective-permute-done.2 = f32[2,16,32,8]{3,2,1,0:T(8,128)} collective-permute-done((f32[2,16,32,8]{3,2,1,0:T(8,128)}, f32[2,16,32,8]{3,2,1,0:T(8,128)}, u32[]{:S(2)}, u32[]{:S(2)}) %collective-permute-start.2) | collective-permute-done | bytes 32800 | tf_op jit(solution)/shard_map/ppermute | solution.py:16
  65.7 3.9 add_select_fusion
  100.4 9.3 %multiply_subtract_fusion.2 = f32[2,16,30,142]{3,2,1,0:T(8,128)S(1)} fusion(f32[2,16,32,144]{3,2,1,0:T(8,128)S(1)} %pad_maximum_fusion.2, f32[2,16,30,142]{3,2,1,0:T(8,128)} %subtract_add_fusion.2, f32[]{:T(128)} %bitcast.5, f32[30,142]{1,0:T(8,128)} %slice.2712, f32[16,30,142]{2,1,0:T(8,128)} %copy.539, f32[16,30,142]{2,1,0:T(8,128)} %copy.538, ...), kind=kLoop, calls=%fused_computation.430 | loop fusion | flops 7906560 | bytes 19227284 | tf_op jit(solution)/shard_map/sub | solution.py:134
  113.1 3.3 add_select_fusion.1
  146.5 9.2 %multiply_subtract_fusion.1 = f32[2,16,28,140]{3,2,1,0:T(8,128)S(1)} fusion(f32[2,16,30,142]{3,2,1,0:T(8,128)S(1)} %multiply_subtract_fusion.2, f32[2,16,28,140]{3,2,1,0:T(8,128)} %subtract_add_fusion.1, f32[]{:T(128)} %bitcast.8, f32[28,140]{1,0:T(8,128)S(1)} %slice.2734, f32[16,28,140]{2,1,0:T(8,128)} %copy.567, f32[16,28,140]{2,1,0:T(8,128)} %copy.566, ...), kind=kLoop, calls=%fused_computation.428 | loop fusion | flops 7275520 | bytes 18546692 | tf_op jit(solution)/shard_map/sub | solution.py:134
  159.0 3.0 add_select_fusion.2
  191.5 9.4 %multiply_subtract_fusion = f32[2,16,26,138]{3,2,1,0:T(8,128)S(1)} fusion(f32[2,16,28,140]{3,2,1,0:T(8,128)S(1)} %multiply_subtract_fusion.1, f32[2,16,26,138]{3,2,1,0:T(8,128)} %subtract_add_fusion, f32[]{:T(128)} %bitcast.11, f32[26,138]{1,0:T(8,128)S(1)} %slice.2755, f32[16,26,138]{2,1,0:T(8,128)} %copy.595, f32[16,26,138]{2,1,0:T(8,128)} %copy.594, ...), kind=kLoop, calls=%fused_computation.426 | loop fusion | flops 6659328 | bytes 17866756 | tf_op jit(solution)/shard_map/sub | solution.py:134
  202.1 2.7 add_select_fusion.3
  222.1 6.2 %multiply_subtract_fusion.6 = f32[2,16,24,136]{3,2,1,0:T(8,128)S(1)} fusion(f32[2,16,26,138]{3,2,1,0:T(8,128)S(1)} %multiply_subtract_fusion, f32[2,16,24,136]{3,2,1,0:T(8,128)S(1)} %subtract_add_fusion.6, f32[]{:T(128)} %bitcast.14, f32[24,136]{1,0:T(8,128)S(1)} %copy-done.17, f32[16,24,136]{2,1,0:T(8,128)S(1)} %copy.623, f32[16,24,136]{2,1,0:T(8,128)S(1)} %copy.622, ...), kind=kLoop, calls=%fused_computation.710 | loop fusion | flops 6057984 | bytes 18890756 | tf_op jit(solution)/shard_map/sub | solution.py:134
  229.1 2.5 add_select_fusion.4
  237.9 4.8 %multiply_subtract_fusion.5 = f32[2,16,22,134]{3,2,1,0:T(8,128)S(1)} fusion(f32[2,16,24,136]{3,2,1,0:T(8,128)S(1)} %multiply_subtract_fusion.6, f32[2,16,22,134]{3,2,1,0:T(8,128)S(1)} %subtract_add_fusion.5, f32[]{:T(128)} %bitcast.17, f32[22,134]{1,0:T(8,128)S(1)} %copy-done.16, f32[16,22,134]{2,1,0:T(8,128)S(1)} %copy.651, f32[16,22,134]{2,1,0:T(8,128)S(1)} %copy.650, ...), kind=kLoop, calls=%fused_computation.708 | loop fusion | flops 5471488 | bytes 20062724 | tf_op jit(solution)/shard_map/sub | solution.py:134
  243.5 2.3 add_select_fusion.5
  251.6 5.1 %multiply_subtract_fusion.4 = f32[2,16,20,132]{3,2,1,0:T(8,128)S(1)} fusion(f32[2,16,22,134]{3,2,1,0:T(8,128)S(1)} %multiply_subtract_fusion.5, f32[2,16,20,132]{3,2,1,0:T(8,128)S(1)} %subtract_add_fusion.4, f32[]{:T(128)} %bitcast.20, f32[20,132]{1,0:T(8,128)S(1)} %copy-done.15, f32[16,20,132]{2,1,0:T(8,128)S(1)} %copy.679, f32[16,20,132]{2,1,0:T(8,128)S(1)} %copy.678, ...), kind=kLoop, calls=%fused_computation.706 | loop fusion | flops 4899840 | bytes 20023300 | tf_op jit(solution)/shard_map/sub | solution.py:134
  264.6 4.8 %multiply_subtract_fusion.3 = f32[2,16,18,130]{3,2,1,0:T(8,128)S(1)} fusion(f32[2,16,20,132]{3,2,1,0:T(8,128)S(1)} %multiply_subtract_fusion.4, f32[2,16,18,130]{3,2,1,0:T(8,128)S(1)} %subtract_add_fusion.3, f32[]{:T(128)} %bitcast.23, f32[18,130]{1,0:T(8,128)S(1)} %copy-done.14, f32[16,18,130]{2,1,0:T(8,128)S(1)} %copy.707, f32[16,18,130]{2,1,0:T(8,128)S(1)} %copy.706, ...), kind=kLoop, calls=%fused_computation.704 | loop fusion | flops 4343040 | bytes 19984900 | tf_op jit(solution)/shard_map/sub | solution.py:134
  274.0 8.0 %stack.71 = f32[9,2,16,16,128]{4,0,3,2,1:T(8,128)} concatenate(f32[1,2,16,16,128]{4,0,3,2,1:T(1,128)S(1)} %bitcast.330, f32[1,2,16,16,128]{4,0,3,2,1:T(1,128)S(1)} %bitcast.336, f32[1,2,16,16,128]{4,0,3,2,1:T(1,128)S(1)} %bitcast.338, f32[1,2,16,16,128]{4,0,3,2,1:T(1,128)S(1)} %bitcast.340, f32[1,2,16,16,128]{4,0,3,2,1:T(1,128)S(1)} %bitcast.342, ...), dimensions={0} | concatenate | bytes 4718592 | tf_op jit(solution)/shard_map/stack | solution.py:144
  282.0 9.0 %convolution_bitcast_fusion = f32[9,9]{0,1:T(8,128)S(1)} fusion(f32[9,2,16,16,128]{4,0,3,2,1:T(8,128)} %stack.71), kind=kOutput, calls=%fused_computation.146 | convolution fusion | flops 63700992 | bytes 2359620 | tf_op jit(solution)/shard_map/dot_general | solution.py:140
  291.1 40.6 %psum.14 = f32[9,9]{0,1:T(8,128)S(1)} all-reduce(f32[9,9]{0,1:T(8,128)S(1)} %convolution_bitcast_fusion), channel_id=1, replica_groups=mesh['gx'=4,'gy'=8] {'gx','gy'}, use_global_device_ids=true, to_apply=%region_0.1 | all-reduce | flops 81 | bytes 648 | tf_op jit(solution)/shard_map/psum | solution.py:141
  334.6 2.6 subtract_divide_fusion.1
  347.5 8.1 %stack.81 = f32[9,65536]{1,0:T(8,128)} concatenate(f32[1,65536]{1,0:T(1,128)S(1)} %bitcast.331, f32[1,65536]{1,0:T(1,128)S(1)} %bitcast.337, f32[1,65536]{1,0:T(1,128)S(1)} %bitcast.339, f32[1,65536]{1,0:T(1,128)S(1)} %bitcast.341, f32[1,65536]{1,0:T(1,128)S(1)} %bitcast.343, f32[1,65536]{1,0:T(1,128)S(1)} %bitcast.345, f32[1,65536]{1,0:T(1,128)S(1)} %bitcast.347, ...), dimensions={0} | concatenate | bytes 4718592 | tf_op jit(solution)/shard_map/stack | solution.py:144
  355.6 5.4 %fusion.1195 = f32[9,65536]{1,0:T(8,128)S(1)} fusion(f32[9,9]{1,0:T(8,128)S(1)} %scatter.74, f32[9,65536]{1,0:T(8,128)} %stack.81), kind=kOutput, calls=%fused_computation.1486 | convolution fusion | flops 63700992 | bytes 4718916 | tf_op jit(solution)/shard_map/dot_general | solution.py:96
  362.9 5.6 %fusion.1196 = f32[9,9]{0,1:T(8,128)S(1)} fusion(f32[9,65536]{1,0:T(8,128)S(1)} %fusion.1195), kind=kOutput, calls=%fused_computation.1487 | convolution fusion | flops 63700992 | bytes 2359620 | tf_op jit(solution)/shard_map/dot_general | solution.py:140
  368.5 40.6 %psum.15 = f32[9,9]{0,1:T(8,128)S(1)} all-reduce(f32[9,9]{0,1:T(8,128)S(1)} %fusion.1196), channel_id=1, replica_groups=mesh['gx'=4,'gy'=8] {'gx','gy'}, use_global_device_ids=true, to_apply=%region_3.5 | all-reduce | flops 81 | bytes 648 | tf_op jit(solution)/shard_map/psum | solution.py:141
  412.9 2.6 subtract_divide_fusion
  425.7 5.4 %fusion.1197 = f32[9,65536]{1,0:T(8,128)S(1)} fusion(f32[9,9]{1,0:T(8,128)S(1)} %scatter.89, f32[9,65536]{1,0:T(8,128)} %copy-done), kind=kOutput, calls=%fused_computation.1488 | convolution fusion | flops 63700992 | bytes 4718916 | tf_op jit(solution)/shard_map/dot_general | solution.py:96
  (407 shorter events, 200.4 us)
Async XLA Ops:
  1.6 25.0 %collective-permute-start = (f32[2,16,8,128]{3,2,1,0:T(8,128)S(1)}, f32[2,16,8,128]{3,2,1,0:T(8,128)S(1)}, u32[]{:S(2)}, u32[]{:S(2)}) collective-permute-start(f32[2,16,8,128]{3,2,1,0:T(8,128)S(1)} %get-tuple-element.464), channel_id=1, source_target_pairs={{0,8},{8,16},{16,24},{1,9},{9,17},{17,25},{2,10},{10,18},{18,26},{... | collective-permute-start | bytes 393224 | tf_op jit(solution)/shard_map/ppermute | solution.py:16
  4.0 22.7 %collective-permute-start.1 = (f32[2,16,8,128]{3,2,1,0:T(8,128)S(1)}, f32[2,16,8,128]{3,2,1,0:T(8,128)S(1)}, u32[]{:S(2)}, u32[]{:S(2)}) collective-permute-start(f32[2,16,8,128]{3,2,1,0:T(8,128)S(1)} %get-tuple-element.463), channel_id=1, source_target_pairs={{8,0},{16,8},{24,16},{9,1},{17,9},{25,17},{10,2},{18,10},{26,18},{... | collective-permute-start | bytes 393224 | tf_op jit(solution)/shard_map/ppermute | solution.py:17
  6.4 19.5 %copy-start.23 = (f32[8]{0:T(128)S(1)}, f32[8]{0:T(128)}, u32[]{:S(2)}) copy-start(f32[8]{0:T(128)} %param.44) | copy-start | bytes 100
  6.4 20.2 %copy-start.1 = (f32[2,16,16,128]{3,2,1,0:T(8,128)S(1)}, f32[2,16,16,128]{3,2,1,0:T(8,128)}, u32[]{:S(2)}) copy-start(f32[2,16,16,128]{3,2,1,0:T(8,128)} %param.41) | copy-start | bytes 786436
  6.5 28.0 %collective-permute-start.5 = (f32[2,16,9,128]{3,1,2,0:T(8,128)S(1)}, f32[2,16,9,128]{3,1,2,0:T(8,128)S(1)}, u32[]{:S(2)}, u32[]{:S(2)}) collective-permute-start(f32[2,16,9,128]{3,1,2,0:T(8,128)S(1)} %copy.751), channel_id=1, source_target_pairs={{8,0},{16,8},{24,16},{9,1},{17,9},{25,17},{10,2},{18,10},{26,18},{... | collective-permute-start | bytes 442376 | tf_op jit(solution)/shard_map/ppermute | solution.py:17
  8.0 28.6 %collective-permute-start.4 = (f32[2,16,9,128]{3,1,2,0:T(8,128)S(1)}, f32[2,16,9,128]{3,1,2,0:T(8,128)S(1)}, u32[]{:S(2)}, u32[]{:S(2)}) collective-permute-start(f32[2,16,9,128]{3,1,2,0:T(8,128)S(1)} %copy.750), channel_id=1, source_target_pairs={{0,8},{8,16},{16,24},{1,9},{9,17},{17,25},{2,10},{10,18},{18,26},{... | collective-permute-start | bytes 442376 | tf_op jit(solution)/shard_map/ppermute | solution.py:16
  27.9 24.0 %collective-permute-start.3 = (f32[2,16,32,8]{3,2,1,0:T(8,128)}, f32[2,16,32,8]{3,2,1,0:T(8,128)S(1)}, u32[]{:S(2)}, u32[]{:S(2)}) collective-permute-start(f32[2,16,32,8]{3,2,1,0:T(8,128)} %get-tuple-element.460), channel_id=1, source_target_pairs={{1,0},{2,1},{3,2},{4,3},{5,4},{6,5},{7,6},{9,8},{10,9},{11,10},{12... | collective-permute-start | bytes 98312 | tf_op jit(solution)/shard_map/ppermute | solution.py:17
  29.2 30.0 %collective-permute-start.2 = (f32[2,16,32,8]{3,2,1,0:T(8,128)}, f32[2,16,32,8]{3,2,1,0:T(8,128)}, u32[]{:S(2)}, u32[]{:S(2)}) collective-permute-start(f32[2,16,32,8]{3,2,1,0:T(8,128)} %get-tuple-element.459), channel_id=1, source_target_pairs={{0,1},{1,2},{2,3},{3,4},{4,5},{5,6},{6,7},{8,9},{9,10},{10,11},{11... | collective-permute-start | bytes 98312 | tf_op jit(solution)/shard_map/ppermute | solution.py:16
  45.3 16.9 %collective-permute-start.7 = (f32[2,16,34,9]{2,1,3,0:T(8,128)}, f32[2,16,34,9]{2,1,3,0:T(8,128)S(1)}, u32[]{:S(2)}, u32[]{:S(2)}) collective-permute-start(f32[2,16,34,9]{2,1,3,0:T(8,128)} %get-tuple-element.440), channel_id=1, source_target_pairs={{1,0},{2,1},{3,2},{4,3},{5,4},{6,5},{7,6},{9,8},{10,9},{11,10},{12... | collective-permute-start | bytes 117512 | tf_op jit(solution)/shard_map/ppermute | solution.py:17
  46.6 16.0 %collective-permute-start.6 = (f32[2,16,34,9]{2,1,3,0:T(8,128)}, f32[2,16,34,9]{2,1,3,0:T(8,128)}, u32[]{:S(2)}, u32[]{:S(2)}) collective-permute-start(f32[2,16,34,9]{2,1,3,0:T(8,128)} %get-tuple-element.439), channel_id=1, source_target_pairs={{0,1},{1,2},{2,3},{3,4},{4,5},{5,6},{6,7},{8,9},{9,10},{10,11},{11... | collective-permute-start | bytes 117512 | tf_op jit(solution)/shard_map/ppermute | solution.py:16
  60.6 3.3 copy-start.4
  64.4 1.3 copy-start.21
  110.5 2.6 copy-start.5
  156.5 2.5 copy-start.6
  201.1 1.0 copy-start.7
  217.6 4.4 %copy-start.8 = (f32[16,24,136]{2,1,0:T(8,128)S(1)}, f32[16,24,136]{2,1,0:T(8,128)}, u32[]{:S(2)}) copy-start(f32[16,24,136]{2,1,0:T(8,128)} %copy.611) | copy-start | bytes 626692
  217.6 4.4 %copy-start.9 = (f32[16,24,136]{2,1,0:T(8,128)S(1)}, f32[16,24,136]{2,1,0:T(8,128)}, u32[]{:S(2)}) copy-start(f32[16,24,136]{2,1,0:T(8,128)} %copy.610) | copy-start | bytes 626692
  217.6 4.4 %copy-start.10 = (f32[16,24,136]{2,1,0:T(8,128)S(1)}, f32[16,24,136]{2,1,0:T(8,128)}, u32[]{:S(2)}) copy-start(f32[16,24,136]{2,1,0:T(8,128)} %copy.609) | copy-start | bytes 626692
  217.6 4.4 %copy-start.17 = (f32[24,136]{1,0:T(8,128)S(1)}, f32[24,136]{1,0:T(8,128)}, u32[]{:S(2)}) copy-start(f32[24,136]{1,0:T(8,128)} %slice.2776) | copy-start | bytes 39172
  218.6 3.5 copy-start.11
  219.6 2.5 copy-start.12
  220.5 1.5 copy-start.13
  236.6 1.3 copy-start.16
  250.1 1.4 copy-start.15
  263.3 1.3 copy-start.14
  264.6 5.1 %copy-start.28 = (pred[16,128]{1,0:T(8,128)(4,1)S(1)}, pred[16,128]{1,0:T(8,128)(4,1)}, u32[]{:S(2)}) copy-start(pred[16,128]{1,0:T(8,128)(4,1)} %broadcast_compare_fusion.7) | copy-start | bytes 6148
  272.1 1.9 copy-start.2
  272.1 1.9 copy-start.3
  333.9 3.3 copy-start.18
  360.9 2.0 copy-start
  362.9 49.2 %copy-start.19 = (f32[9,9]{1,0:T(8,128)S(1)}, f32[9,9]{1,0:T(8,128)}, u32[]{:S(2)}) copy-start(f32[9,9]{1,0:T(8,128)} %copy-done.18) | copy-start | bytes 976
  411.4 4.2 copy-start.20
  (5 other events, 4.1 us)
where the time goes:
time: 442 us; the launch traced here: 434 us
  local copies, waits for them, and re-layouts  168 us (38%)
  other arithmetic  104 us (24%)
  blocking collectives  81.2 us (18%)
  matrix products  46.2 us (10%)
  starting transfers between devices  24 us (5%)
  waiting for transfers between devices  7.31 us (2%)
    mul x208, local copies, waits for them, and re-layouts, apply_operator(): weight * 0.5  117 us
    psum x2, blocking collectives, global_gram(): summed = lax.psum(partial_value, ('gx', 'gy'))  81.2 us
    sub x8, other arithmetic, on_device(): current = applied - shifts[power] * current[:, :, 1:-1, 1:-1]  50.7 us
    select_n x8, other arithmetic, apply_operator(): safe_diag = jnp.where(region_mask > 0, diagonal, 1.0)  20.3 us
    dot_general x14, matrix products, lower_inverse(): jnp.dot(factor_low[position, :position], inverse[:position], precision=la...  20 us
    ppermute x4, starting transfers between devices, extended(): before = lax.ppermute(last, axis, up)  18.7 us
    another operation x2, local copies, waits for them, and re-layouts, on_device(): basis_rows = jnp.stack(krylov).reshape(powers + 1, -1)  16.1 us
    dot_general x2, matrix products, global_gram(): jnp.dot(basis_rows, basis_rows.T, precision=lax.Precision.HIGHEST)  14.7 us
  transfers between devices with their start and end apart: 8, of which 1 were waited for; matrix products, arithmetic and copies ran while one was open for 7% of the time, Pallas kernels for 0%

commit v1 on v0

--- a/solution.py
+++ b/solution.py
@@ -138,7 +138,9 @@
 
     def global_gram(basis_rows):
         partial_value = jnp.dot(basis_rows, basis_rows.T, precision=lax.Precision.HIGHEST)
-        summed = lax.psum(partial_value, ("gx", "gy"))
+        summed = partial_value
+        for mesh_axis in ("gy", "gx"):
+            summed = lax.psum(summed, mesh_axis)
         return summed / total_count
 
     basis_rows = jnp.stack(krylov).reshape(powers + 1, -1)

time: 442 us -> 412 us (0.932)
  blocking collectives: 81.2 us -> 49.2 us
    psum x2 -> x4, blocking collectives: 81.2 us -> 49.2 us  [global_gram(): summed = lax.psum(summed, mesh_axis)]
where the time goes in v1:
time: 412 us; the launch traced here: 404 us
  local copies, waits for them, and re-layouts  168 us (41%)
  other arithmetic  106 us (26%)
  blocking collectives  49.2 us (12%)
  matrix products  46.5 us (11%)
  starting transfers between devices  23.4 us (6%)
  waiting for transfers between devices  8.77 us (2%)
    mul x208, local copies, waits for them, and re-layouts, apply_operator(): weight * 0.5  118 us
    sub x8, other arithmetic, on_device(): current = applied - shifts[power] * current[:, :, 1:-1, 1:-1]  50.9 us
    psum x4, blocking collectives, global_gram(): summed = lax.psum(summed, mesh_axis)  49.2 us
    dot_general x14, matrix products, lower_inverse(): jnp.dot(factor_low[position, :position], inverse[:position], precision=la...  20.3 us
    select_n x8, other arithmetic, apply_operator(): safe_diag = jnp.where(region_mask > 0, diagonal, 1.0)  20.2 us
    ppermute x4, starting transfers between devices, extended(): before = lax.ppermute(last, axis, up)  18.1 us
    another operation x2, local copies, waits for them, and re-layouts, on_device(): basis_rows = jnp.stack(krylov).reshape(powers + 1, -1)  16 us
    dot_general x2, matrix products, global_gram(): jnp.dot(basis_rows, basis_rows.T, precision=lax.Precision.HIGHEST)  14.6 us
  transfers between devices with their start and end apart: 8, of which 1 were waited for; matrix products, arithmetic and copies ran while one was open for 7% of the time, Pallas kernels for 0%

profile of v1, /device:TPU:0, one launch (start us, length us, event | category | flops | bytes accessed | tf_op | source)
XLA Modules:
  0.0 404.1 jit_solution(13354014796773766593)
XLA Ops:
  1.6 2.4 collective-permute-start
  8.0 5.8 %collective-permute-start.4 = (f32[2,16,9,128]{3,1,2,0:T(8,128)S(1)}, f32[2,16,9,128]{3,1,2,0:T(8,128)S(1)}, u32[]{:S(2)}, u32[]{:S(2)}) collective-permute-start(f32[2,16,9,128]{3,1,2,0:T(8,128)S(1)} %copy.750), channel_id=1, source_target_pairs={{0,8},{8,16},{16,24},{1,9},{9,17},{17,25},{2,10},{10,18},{18,26},{... | collective-permute-start | bytes 442376 | tf_op jit(solution)/shard_map/ppermute | solution.py:16
  29.1 5.4 %collective-permute-start.2 = (f32[2,16,32,8]{3,2,1,0:T(8,128)}, f32[2,16,32,8]{3,2,1,0:T(8,128)}, u32[]{:S(2)}, u32[]{:S(2)}) collective-permute-start(f32[2,16,32,8]{3,2,1,0:T(8,128)} %get-tuple-element.459), channel_id=1, source_target_pairs={{0,1},{1,2},{2,3},{3,4},{4,5},{5,6},{6,7},{8,9},{9,10},{10,11},{11... | collective-permute-start | bytes 98312 | tf_op jit(solution)/shard_map/ppermute | solution.py:16
  36.6 2.2 copy.506
  38.8 4.0 pad_maximum_fusion
  45.8 4.6 %collective-permute-start.6 = (f32[2,16,34,9]{2,1,3,0:T(8,128)}, f32[2,16,34,9]{2,1,3,0:T(8,128)S(1)}, u32[]{:S(2)}, u32[]{:S(2)}) collective-permute-start(f32[2,16,34,9]{2,1,3,0:T(8,128)} %get-tuple-element.439), channel_id=1, source_target_pairs={{0,1},{1,2},{2,3},{3,4},{4,5},{5,6},{6,7},{8,9},{9,10},{10,11},{11... | collective-permute-start | bytes 117512 | tf_op jit(solution)/shard_map/ppermute | solution.py:16
  50.4 8.8 %collective-permute-done.2 = f32[2,16,32,8]{3,2,1,0:T(8,128)} collective-permute-done((f32[2,16,32,8]{3,2,1,0:T(8,128)}, f32[2,16,32,8]{3,2,1,0:T(8,128)}, u32[]{:S(2)}, u32[]{:S(2)}) %collective-permute-start.2) | collective-permute-done | bytes 32800 | tf_op jit(solution)/shard_map/ppermute | solution.py:16
  66.8 3.9 add_select_fusion
  101.4 9.3 %multiply_subtract_fusion.2 = f32[2,16,30,142]{3,2,1,0:T(8,128)S(1)} fusion(f32[2,16,32,144]{3,2,1,0:T(8,128)S(1)} %pad_maximum_fusion.2, f32[2,16,30,142]{3,2,1,0:T(8,128)} %subtract_add_fusion.2, f32[]{:T(128)} %bitcast.5, f32[30,142]{1,0:T(8,128)} %slice.2712, f32[16,30,142]{2,1,0:T(8,128)} %copy.539, f32[16,30,142]{2,1,0:T(8,128)} %copy.538, ...), kind=kLoop, calls=%fused_computation.430 | loop fusion | flops 7906560 | bytes 19227284 | tf_op jit(solution)/shard_map/sub | solution.py:134
  114.1 3.3 add_select_fusion.1
  147.3 9.3 %multiply_subtract_fusion.1 = f32[2,16,28,140]{3,2,1,0:T(8,128)S(1)} fusion(f32[2,16,30,142]{3,2,1,0:T(8,128)S(1)} %multiply_subtract_fusion.2, f32[2,16,28,140]{3,2,1,0:T(8,128)} %subtract_add_fusion.1, f32[]{:T(128)} %bitcast.8, f32[28,140]{1,0:T(8,128)S(1)} %slice.2734, f32[16,28,140]{2,1,0:T(8,128)} %copy.567, f32[16,28,140]{2,1,0:T(8,128)} %copy.566, ...), kind=kLoop, calls=%fused_computation.428 | loop fusion | flops 7275520 | bytes 18546692 | tf_op jit(solution)/shard_map/sub | solution.py:134
  160.0 3.0 add_select_fusion.2
  192.5 9.5 %multiply_subtract_fusion = f32[2,16,26,138]{3,2,1,0:T(8,128)S(1)} fusion(f32[2,16,28,140]{3,2,1,0:T(8,128)S(1)} %multiply_subtract_fusion.1, f32[2,16,26,138]{3,2,1,0:T(8,128)} %subtract_add_fusion, f32[]{:T(128)} %bitcast.11, f32[26,138]{1,0:T(8,128)S(1)} %slice.2755, f32[16,26,138]{2,1,0:T(8,128)} %copy.595, f32[16,26,138]{2,1,0:T(8,128)} %copy.594, ...), kind=kLoop, calls=%fused_computation.426 | loop fusion | flops 6659328 | bytes 17866756 | tf_op jit(solution)/shard_map/sub | solution.py:134
  203.1 2.7 add_select_fusion.3
  223.9 6.2 %multiply_subtract_fusion.6 = f32[2,16,24,136]{3,2,1,0:T(8,128)S(1)} fusion(f32[2,16,26,138]{3,2,1,0:T(8,128)S(1)} %multiply_subtract_fusion, f32[2,16,24,136]{3,2,1,0:T(8,128)S(1)} %subtract_add_fusion.6, f32[]{:T(128)} %bitcast.14, f32[24,136]{1,0:T(8,128)S(1)} %copy-done.17, f32[16,24,136]{2,1,0:T(8,128)S(1)} %copy.623, f32[16,24,136]{2,1,0:T(8,128)S(1)} %copy.622, ...), kind=kLoop, calls=%fused_computation.710 | loop fusion | flops 6057984 | bytes 18706436 | tf_op jit(solution)/shard_map/sub | solution.py:134
  230.9 2.5 add_select_fusion.4
  239.7 4.9 %multiply_subtract_fusion.5 = f32[2,16,22,134]{3,2,1,0:T(8,128)S(1)} fusion(f32[2,16,24,136]{3,2,1,0:T(8,128)S(1)} %multiply_subtract_fusion.6, f32[2,16,22,134]{3,2,1,0:T(8,128)S(1)} %subtract_add_fusion.5, f32[]{:T(128)} %bitcast.17, f32[22,134]{1,0:T(8,128)S(1)} %copy-done.16, f32[16,22,134]{2,1,0:T(8,128)S(1)} %copy.651, f32[16,22,134]{2,1,0:T(8,128)S(1)} %copy.650, ...), kind=kLoop, calls=%fused_computation.708 | loop fusion | flops 5471488 | bytes 20062724 | tf_op jit(solution)/shard_map/sub | solution.py:134
  245.4 2.3 add_select_fusion.5
  253.4 5.0 %multiply_subtract_fusion.4 = f32[2,16,20,132]{3,2,1,0:T(8,128)S(1)} fusion(f32[2,16,22,134]{3,2,1,0:T(8,128)S(1)} %multiply_subtract_fusion.5, f32[2,16,20,132]{3,2,1,0:T(8,128)S(1)} %subtract_add_fusion.4, f32[]{:T(128)} %bitcast.20, f32[20,132]{1,0:T(8,128)S(1)} %copy-done.15, f32[16,20,132]{2,1,0:T(8,128)S(1)} %copy.679, f32[16,20,132]{2,1,0:T(8,128)S(1)} %copy.678, ...), kind=kLoop, calls=%fused_computation.706 | loop fusion | flops 4899840 | bytes 20023300 | tf_op jit(solution)/shard_map/sub | solution.py:134
  267.0 4.8 %multiply_subtract_fusion.3 = f32[2,16,18,130]{3,2,1,0:T(8,128)S(1)} fusion(f32[2,16,20,132]{3,2,1,0:T(8,128)S(1)} %multiply_subtract_fusion.4, f32[2,16,18,130]{3,2,1,0:T(8,128)S(1)} %subtract_add_fusion.3, f32[]{:T(128)} %bitcast.23, f32[18,130]{1,0:T(8,128)S(1)} %copy-done.14, f32[16,18,130]{2,1,0:T(8,128)S(1)} %copy.707, f32[16,18,130]{2,1,0:T(8,128)S(1)} %copy.706, ...), kind=kLoop, calls=%fused_computation.704 | loop fusion | flops 4343040 | bytes 19984900 | tf_op jit(solution)/shard_map/sub | solution.py:134
  276.4 8.0 %stack.71 = f32[9,2,16,16,128]{4,0,3,2,1:T(8,128)} concatenate(f32[1,2,16,16,128]{4,0,3,2,1:T(1,128)S(1)} %bitcast.330, f32[1,2,16,16,128]{4,0,3,2,1:T(1,128)S(1)} %bitcast.336, f32[1,2,16,16,128]{4,0,3,2,1:T(1,128)S(1)} %bitcast.338, f32[1,2,16,16,128]{4,0,3,2,1:T(1,128)S(1)} %bitcast.340, f32[1,2,16,16,128]{4,0,3,2,1:T(1,128)S(1)} %bitcast.342, ...), dimensions={0} | concatenate | bytes 4718592 | tf_op jit(solution)/shard_map/stack | solution.py:146
  284.4 9.0 %convolution_bitcast_fusion = f32[9,9]{0,1:T(8,128)S(1)} fusion(f32[9,2,16,16,128]{4,0,3,2,1:T(8,128)} %stack.71), kind=kOutput, calls=%fused_computation.146 | convolution fusion | flops 63700992 | bytes 2359620 | tf_op jit(solution)/shard_map/dot_general | solution.py:140
  293.4 20.1 %psum.28 = f32[9,9]{0,1:T(8,128)S(1)} all-reduce(f32[9,9]{0,1:T(8,128)S(1)} %convolution_bitcast_fusion), channel_id=1, replica_groups=mesh['gx'=4,'gy'=8] {'gy'}, use_global_device_ids=true, to_apply=%region_0.1 | all-reduce | flops 81 | bytes 648 | tf_op jit(solution)/shard_map/psum | solution.py:143
  313.5 5.8 %psum.29 = f32[9,9]{0,1:T(8,128)S(1)} all-reduce(f32[9,9]{0,1:T(8,128)S(1)} %psum.28), channel_id=1, replica_groups=mesh['gx'=4,'gy'=8] {'gx'}, use_global_device_ids=true, to_apply=%region_1.2 | all-reduce | flops 81 | bytes 648 | tf_op jit(solution)/shard_map/psum | solution.py:143
  322.3 2.5 subtract_divide_fusion.1
  335.1 8.0 %stack.81 = f32[9,65536]{1,0:T(8,128)} concatenate(f32[1,65536]{1,0:T(1,128)S(1)} %bitcast.331, f32[1,65536]{1,0:T(1,128)S(1)} %bitcast.337, f32[1,65536]{1,0:T(1,128)S(1)} %bitcast.339, f32[1,65536]{1,0:T(1,128)S(1)} %bitcast.341, f32[1,65536]{1,0:T(1,128)S(1)} %bitcast.343, f32[1,65536]{1,0:T(1,128)S(1)} %bitcast.345, f32[1,65536]{1,0:T(1,128)S(1)} %bitcast.347, ...), dimensions={0} | concatenate | bytes 4718592 | tf_op jit(solution)/shard_map/stack | solution.py:146
  343.2 5.4 %fusion.1195 = f32[9,65536]{1,0:T(8,128)S(1)} fusion(f32[9,9]{1,0:T(8,128)S(1)} %scatter.74, f32[9,65536]{1,0:T(8,128)} %stack.81), kind=kOutput, calls=%fused_computation.1486 | convolution fusion | flops 63700992 | bytes 4718916 | tf_op jit(solution)/shard_map/dot_general | solution.py:96
  350.5 5.6 %fusion.1196 = f32[9,9]{0,1:T(8,128)S(1)} fusion(f32[9,65536]{1,0:T(8,128)S(1)} %fusion.1195), kind=kOutput, calls=%fused_computation.1487 | convolution fusion | flops 63700992 | bytes 2359620 | tf_op jit(solution)/shard_map/dot_general | solution.py:140
  356.1 17.4 %psum.30 = f32[9,9]{0,1:T(8,128)S(1)} all-reduce(f32[9,9]{0,1:T(8,128)S(1)} %fusion.1196), channel_id=1, replica_groups=mesh['gx'=4,'gy'=8] {'gy'}, use_global_device_ids=true, to_apply=%region_4.6 | all-reduce | flops 81 | bytes 648 | tf_op jit(solution)/shard_map/psum | solution.py:143
  373.5 5.9 %psum.31 = f32[9,9]{0,1:T(8,128)S(1)} all-reduce(f32[9,9]{0,1:T(8,128)S(1)} %psum.30), channel_id=1, replica_groups=mesh['gx'=4,'gy'=8] {'gx'}, use_global_device_ids=true, to_apply=%region_5.7 | all-reduce | flops 81 | bytes 648 | tf_op jit(solution)/shard_map/psum | solution.py:143
  383.2 2.5 subtract_divide_fusion
  396.1 5.4 %fusion.1197 = f32[9,65536]{1,0:T(8,128)S(1)} fusion(f32[9,9]{1,0:T(8,128)S(1)} %scatter.89, f32[9,65536]{1,0:T(8,128)} %copy-done), kind=kOutput, calls=%fused_computation.1488 | convolution fusion | flops 63700992 | bytes 4718916 | tf_op jit(solution)/shard_map/dot_general | solution.py:96
  (409 shorter events, 206.5 us)
Async XLA Ops:
  1.6 25.0 %collective-permute-start = (f32[2,16,8,128]{3,2,1,0:T(8,128)S(1)}, f32[2,16,8,128]{3,2,1,0:T(8,128)S(1)}, u32[]{:S(2)}, u32[]{:S(2)}) collective-permute-start(f32[2,16,8,128]{3,2,1,0:T(8,128)S(1)} %get-tuple-element.464), channel_id=1, source_target_pairs={{0,8},{8,16},{16,24},{1,9},{9,17},{17,25},{2,10},{10,18},{18,26},{... | collective-permute-start | bytes 393224 | tf_op jit(solution)/shard_map/ppermute | solution.py:16
  4.0 22.7 %collective-permute-start.1 = (f32[2,16,8,128]{3,2,1,0:T(8,128)S(1)}, f32[2,16,8,128]{3,2,1,0:T(8,128)S(1)}, u32[]{:S(2)}, u32[]{:S(2)}) collective-permute-start(f32[2,16,8,128]{3,2,1,0:T(8,128)S(1)} %get-tuple-element.463), channel_id=1, source_target_pairs={{8,0},{16,8},{24,16},{9,1},{17,9},{25,17},{10,2},{18,10},{26,18},{... | collective-permute-start | bytes 393224 | tf_op jit(solution)/shard_map/ppermute | solution.py:17
  6.4 19.5 %copy-start.23 = (f32[8]{0:T(128)S(1)}, f32[8]{0:T(128)}, u32[]{:S(2)}) copy-start(f32[8]{0:T(128)} %param.44) | copy-start | bytes 100
  6.4 20.2 %copy-start.1 = (f32[2,16,16,128]{3,2,1,0:T(8,128)S(1)}, f32[2,16,16,128]{3,2,1,0:T(8,128)}, u32[]{:S(2)}) copy-start(f32[2,16,16,128]{3,2,1,0:T(8,128)} %param.41) | copy-start | bytes 786436
  6.5 28.0 %collective-permute-start.5 = (f32[2,16,9,128]{3,1,2,0:T(8,128)S(1)}, f32[2,16,9,128]{3,1,2,0:T(8,128)S(1)}, u32[]{:S(2)}, u32[]{:S(2)}) collective-permute-start(f32[2,16,9,128]{3,1,2,0:T(8,128)S(1)} %copy.751), channel_id=1, source_target_pairs={{8,0},{16,8},{24,16},{9,1},{17,9},{25,17},{10,2},{18,10},{26,18},{... | collective-permute-start | bytes 442376 | tf_op jit(solution)/shard_map/ppermute | solution.py:17
  8.0 28.6 %collective-permute-start.4 = (f32[2,16,9,128]{3,1,2,0:T(8,128)S(1)}, f32[2,16,9,128]{3,1,2,0:T(8,128)S(1)}, u32[]{:S(2)}, u32[]{:S(2)}) collective-permute-start(f32[2,16,9,128]{3,1,2,0:T(8,128)S(1)} %copy.750), channel_id=1, source_target_pairs={{0,8},{8,16},{16,24},{1,9},{9,17},{17,25},{2,10},{10,18},{18,26},{... | collective-permute-start | bytes 442376 | tf_op jit(solution)/shard_map/ppermute | solution.py:16
  27.9 22.5 %collective-permute-start.3 = (f32[2,16,32,8]{3,2,1,0:T(8,128)}, f32[2,16,32,8]{3,2,1,0:T(8,128)}, u32[]{:S(2)}, u32[]{:S(2)}) collective-permute-start(f32[2,16,32,8]{3,2,1,0:T(8,128)} %get-tuple-element.460), channel_id=1, source_target_pairs={{1,0},{2,1},{3,2},{4,3},{5,4},{6,5},{7,6},{9,8},{10,9},{11,10},{12... | collective-permute-start | bytes 98312 | tf_op jit(solution)/shard_map/ppermute | solution.py:17
  29.1 30.0 %collective-permute-start.2 = (f32[2,16,32,8]{3,2,1,0:T(8,128)}, f32[2,16,32,8]{3,2,1,0:T(8,128)}, u32[]{:S(2)}, u32[]{:S(2)}) collective-permute-start(f32[2,16,32,8]{3,2,1,0:T(8,128)} %get-tuple-element.459), channel_id=1, source_target_pairs={{0,1},{1,2},{2,3},{3,4},{4,5},{5,6},{6,7},{8,9},{9,10},{10,11},{11... | collective-permute-start | bytes 98312 | tf_op jit(solution)/shard_map/ppermute | solution.py:16
  44.5 17.9 %collective-permute-start.7 = (f32[2,16,34,9]{2,1,3,0:T(8,128)}, f32[2,16,34,9]{2,1,3,0:T(8,128)S(1)}, u32[]{:S(2)}, u32[]{:S(2)}) collective-permute-start(f32[2,16,34,9]{2,1,3,0:T(8,128)} %get-tuple-element.440), channel_id=1, source_target_pairs={{1,0},{2,1},{3,2},{4,3},{5,4},{6,5},{7,6},{9,8},{10,9},{11,10},{12... | collective-permute-start | bytes 117512 | tf_op jit(solution)/shard_map/ppermute | solution.py:17
  45.8 17.0 %collective-permute-start.6 = (f32[2,16,34,9]{2,1,3,0:T(8,128)}, f32[2,16,34,9]{2,1,3,0:T(8,128)S(1)}, u32[]{:S(2)}, u32[]{:S(2)}) collective-permute-start(f32[2,16,34,9]{2,1,3,0:T(8,128)} %get-tuple-element.439), channel_id=1, source_target_pairs={{0,1},{1,2},{2,3},{3,4},{4,5},{5,6},{6,7},{8,9},{9,10},{10,11},{11... | collective-permute-start | bytes 117512 | tf_op jit(solution)/shard_map/ppermute | solution.py:16
  65.5 1.3 copy-start.21
  111.5 2.5 copy-start.4
  157.5 2.5 copy-start.5
  202.1 1.0 copy-start.6
  219.3 4.4 %copy-start.7 = (f32[16,24,136]{2,1,0:T(8,128)S(1)}, f32[16,24,136]{2,1,0:T(8,128)}, u32[]{:S(2)}) copy-start(f32[16,24,136]{2,1,0:T(8,128)} %copy.612) | copy-start | bytes 626692
  219.3 4.5 %copy-start.8 = (f32[16,24,136]{2,1,0:T(8,128)S(1)}, f32[16,24,136]{2,1,0:T(8,128)}, u32[]{:S(2)}) copy-start(f32[16,24,136]{2,1,0:T(8,128)} %copy.611) | copy-start | bytes 626692
  219.3 4.5 %copy-start.9 = (f32[16,24,136]{2,1,0:T(8,128)S(1)}, f32[16,24,136]{2,1,0:T(8,128)}, u32[]{:S(2)}) copy-start(f32[16,24,136]{2,1,0:T(8,128)} %copy.610) | copy-start | bytes 626692
  219.3 4.5 %copy-start.17 = (f32[24,136]{1,0:T(8,128)S(1)}, f32[24,136]{1,0:T(8,128)}, u32[]{:S(2)}) copy-start(f32[24,136]{1,0:T(8,128)} %slice.2776) | copy-start | bytes 39172
  220.3 3.5 copy-start.10
  221.3 2.5 copy-start.11
  222.3 1.5 copy-start.12
  238.3 1.3 copy-start.16
  252.0 1.4 copy-start.15
  258.6 1.4 copy-start.24
  265.7 1.3 copy-start.14
  267.0 5.1 %copy-start.28 = (pred[16,128]{1,0:T(8,128)(4,1)S(1)}, pred[16,128]{1,0:T(8,128)(4,1)}, u32[]{:S(2)}) copy-start(pred[16,128]{1,0:T(8,128)(4,1)} %broadcast_compare_fusion.7) | copy-start | bytes 6148
  274.4 2.0 copy-start.2
  274.5 2.0 copy-start.3
  321.6 3.2 copy-start.18
  348.5 2.0 copy-start
  350.5 31.9 %copy-start.19 = (f32[9,9]{1,0:T(8,128)S(1)}, f32[9,9]{1,0:T(8,128)}, u32[]{:S(2)}) copy-start(f32[9,9]{1,0:T(8,128)} %copy-done.18) | copy-start | bytes 976
  381.7 4.1 %copy-start.20 = (f32[9,9]{1,0:T(8,128)}, f32[9,9]{1,0:T(8,128)S(1)}, u32[]{:S(2)}) copy-start(f32[9,9]{1,0:T(8,128)S(1)} %select_select_fusion) | copy-start | bytes 976
  (5 other events, 4.3 us)
